TPU v7x, 32 devices: a whole 2x2x4 slice. The times are simulated.
32 devices in a mesh: dp: 8 (over z, y), tensor: 4 (over x, core).
Axes of the slice: x: 2, y: 2, z: 4, core: 2. Of those that a mesh axis runs over, the one named last changes fastest.
Arguments:
- tokens: bfloat16 [1024, 4096], P(('dp', 'tensor')), may hold values from -6 to 6
- upstream_grad: bfloat16 [1024, 4096], P(('dp', 'tensor')), may hold values from -6 to 6
- w_gate: bfloat16 [4096, 3584], P(None, 'tensor'), may hold values from -0.09375 to 0.09375
- w_up: bfloat16 [4096, 3584], P(None, 'tensor'), may hold values from -0.09375 to 0.09375
- w_down: bfloat16 [3584, 4096], P('tensor'), may hold values from -0.09375 to 0.09375
Outputs:
- grad_tokens: bfloat16 [1024, 4096], P(('dp', 'tensor'))
- grad_down: float32 [3584, 4096], P('tensor', 'dp')
All inputs are finite; a program needn't handle non-finite values.
Results may differ from a plain program's by a relative error of at most 0.03.
Values may be sent and summed in bfloat16 or wider, within the bound.
A program may use at most 128 MiB of HBM per device.

v0:
```python
import jax
import jax.numpy as jnp
from jax import lax
from jax.sharding import PartitionSpec as P


def contract_rows(left, right):
    return lax.dot_general(
        left, right, (((0,), (0,)), ((), ())), preferred_element_type=jnp.float32
    )


def contract_cols(left, right):
    return lax.dot_general(
        left, right, (((1,), (1,)), ((), ())), preferred_element_type=jnp.float32
    )


def body(tokens, upstream_grad, w_gate, w_up, w_down):
    gathered, upstream = (
        lax.all_gather(tokens, "tensor", axis=0, tiled=True),
        lax.all_gather(upstream_grad, "tensor", axis=0, tiled=True),
    )
    gate_pre = jnp.dot(gathered, w_gate, preferred_element_type=jnp.float32)
    up_pre = jnp.dot(gathered, w_up, preferred_element_type=jnp.float32)
    sig_gate = jax.nn.sigmoid(gate_pre)
    act_gate = gate_pre * sig_gate
    hidden = (act_gate * up_pre).astype(jnp.bfloat16)
    grad_hidden = contract_cols(upstream, w_down).astype(jnp.bfloat16)
    hidden_f = grad_hidden.astype(jnp.float32)
    grad_gate = (hidden_f * up_pre * sig_gate * (1.0 + gate_pre * (1.0 - sig_gate))).astype(
        jnp.bfloat16
    )
    grad_up = (hidden_f * act_gate).astype(jnp.bfloat16)
    total_tokens = upstream.shape[0] * lax.axis_size("dp")
    factor = float(total_tokens) ** (-0.5)
    summed = lax.psum_scatter(
        (contract_cols(grad_gate, w_gate) + contract_cols(grad_up, w_up)).astype(jnp.bfloat16),
        "tensor",
        scatter_dimension=0,
        tiled=True,
    )
    partial_grad = contract_rows(hidden, upstream) * factor
    grad_down = lax.psum_scatter(
        partial_grad.astype(jnp.bfloat16), "dp", scatter_dimension=1, tiled=True
    ).astype(jnp.float32)
    return (summed, grad_down)


def solution(mesh):
    in_specs = (
        P(("dp", "tensor"), None),
        P(("dp", "tensor"), None),
        P(None, "tensor"),
        P(None, "tensor"),
        P("tensor", None),
    )
    out_specs = (P(("dp", "tensor"), None), P("tensor", "dp"))
    return jax.shard_map(body, mesh=mesh, in_specs=in_specs, out_specs=out_specs, check_vma=False)
```

profile of v0, /device:TPU:0, one launch (start us, length us, event | category | flops | bytes accessed | tf_op | source)
XLA Modules:
  0.0 220.5 jit_solution(15488147978585439065)
XLA Ops:
  7.2 0.0 all-gather.5.cloned.1.call-start
  7.2 0.7 all-gather.5.cloned.1.call-update
  7.9 0.0 all-gather.3.cloned.1.call-start
  7.9 0.7 all-gather.3.cloned.1.call-update
  8.6 0.0 reduce-scatter.5.cloned.1.call-start
  8.7 20.3 %all-gather.5.cloned.1.call-done = bf16[128,4096]{1,0:T(8,128)(2,1)} async-done(((bf16[32,4096]{1,0:T(8,128)(2,1)}), bf16[128,4096]{1,0:T(8,128)(2,1)}) %all-gather.5.cloned.1.call-update) | async-done | bytes 1048592 | tf_op jit(solution)/shard_map/all_gather | solution.py:21
  29.0 4.8 %fusion.11 = f32[128,896]{1,0:T(8,128)S(1)} fusion(bf16[128,4096]{1,0:T(8,128)(2,1)} %all-gather.5.cloned.1.call-done, bf16[4096,896]{1,0:T(8,128)(2,1)} %param.7), kind=kOutput, calls=%fused_computation.16 | convolution fusion | flops 939524096 | bytes 8847360 | tf_op jit(solution)/shard_map/dot_general | solution.py:24
  33.8 0.0 copy-done
  33.8 4.4 %fusion.10 = f32[128,896]{1,0:T(8,128)S(1)} fusion(bf16[128,4096]{1,0:T(8,128)(2,1)S(1)} %copy-done, bf16[4096,896]{1,0:T(8,128)(2,1)} %param.8), kind=kOutput, calls=%fused_computation.15 | convolution fusion | flops 939524096 | bytes 8847360 | tf_op jit(solution)/shard_map/dot_general | solution.py:25
  38.2 9.1 %all-gather.3.cloned.1.call-done = bf16[128,4096]{1,0:T(8,128)(2,1)} async-done(((bf16[32,4096]{1,0:T(8,128)(2,1)}), bf16[128,4096]{1,0:T(8,128)(2,1)}) %all-gather.3.cloned.1.call-update) | async-done | bytes 1048592 | tf_op jit(solution)/shard_map/all_gather | solution.py:22
  47.3 6.4 %multiply_convert_fusion = bf16[896,4096]{1,0:T(8,128)(2,1)} fusion(bf16[128,4096]{1,0:T(8,128)(2,1)} %all-gather.3.cloned.1.call-done, f32[128,896]{1,0:T(8,128)S(1)} %fusion.10, f32[128,896]{1,0:T(8,128)S(1)} %fusion.11), kind=kOutput, calls=%fused_computation | convolution fusion | flops 947552256 | bytes 9306112 | tf_op jit(solution)/shard_map/dot_general | solution.py:8
  53.7 0.0 reduce-scatter.5.cloned.1.call-update
  53.7 0.0 reduce-scatter.3.cloned.1.call-start
  53.8 0.0 copy-done.1
  53.8 0.0 slice-start
  53.8 5.7 %fusion.1 = f32[128,896]{1,0:T(8,128)S(1)} fusion(bf16[128,4096]{1,0:T(8,128)(2,1)S(1)} %copy-done.1, bf16[896,4096]{1,0:T(8,128)(2,1)} %param.9), kind=kOutput, calls=%fused_computation.4 | convolution fusion | flops 939753472 | bytes 8847360 | tf_op jit(solution)/shard_map/dot_general | solution.py:14
  59.5 0.0 slice-start.1
  59.5 6.3 %fusion.3 = f32[128,4096]{1,0:T(8,128)S(1)} fusion(bf16[4096,896]{1,0:T(8,128)(2,1)} %param.7, f32[128,896]{1,0:T(8,128)S(1)} %fusion.11, f32[128,896]{1,0:T(8,128)S(1)} %fusion.1, f32[128,896]{1,0:T(8,128)S(1)} %fusion.10), kind=kOutput, calls=%fused_computation.10 | convolution fusion | flops 940670976 | bytes 10813440 | tf_op jit(solution)/shard_map/dot_general | solution.py:14
  65.8 0.0 slice-done
  65.9 3.5 %fusion = bf16[128,4096]{1,0:T(8,128)(2,1)} fusion(f32[128,4096]{1,0:T(8,128)S(1)} %fusion.3, bf16[4096,896]{1,0:T(8,128)(2,1)S(1)} %bitcast.10, f32[128,896]{1,0:T(8,128)S(1)} %fusion.1, f32[128,896]{1,0:T(8,128)S(1)} %fusion.11), kind=kOutput, calls=%fused_computation.2 | convolution fusion | flops 941260800 | bytes 11403264 | tf_op jit(solution)/shard_map/dot_general | solution.py:14
  69.3 0.0 reduce-scatter.3.cloned.1.call-update
  69.4 117.6 %reduce-scatter.5.cloned.1.call-done = bf16[896,512]{1,0:T(8,128)(2,1)} async-done(((bf16[896,4096]{1,0:T(8,128)(2,1)}), bf16[896,512]{1,0:T(8,128)(2,1)}) %reduce-scatter.5.cloned.1.call-update) | async-done | bytes 917520 | tf_op jit(solution)/shard_map/reduce_scatter | solution.py:44
  186.9 2.7 %convert_element_type.31 = f32[896,512]{1,0:T(8,128)} convert(bf16[896,512]{1,0:T(8,128)(2,1)} %reduce-scatter.5.cloned.1.call-done) | non-fusion elementwise | flops 458752 | bytes 2752512 | tf_op jit(solution)/shard_map/convert_element_type | solution.py:46
  189.6 24.3 %reduce-scatter.3.cloned.1.call-done = bf16[32,4096]{1,0:T(8,128)(2,1)} async-done(((bf16[128,4096]{1,0:T(8,128)(2,1)}), bf16[32,4096]{1,0:T(8,128)(2,1)}) %reduce-scatter.3.cloned.1.call-update) | async-done | bytes 262160 | tf_op jit(solution)/shard_map/reduce_scatter | solution.py:37
  (4 shorter events, 0.0 us)
Async XLA Ops:
  7.2 21.8 %all-gather.5.cloned.1.call-start = ((), (), s32[]{:S(2)}) async-start(), calls=%async_computation.3 | async-start | bytes 1310720 | tf_op jit(solution)/shard_map/all_gather | solution.py:21
  7.9 39.4 %all-gather.3.cloned.1.call-start = ((), (), s32[]{:S(2)}) async-start(), calls=%async_computation.2 | async-start | bytes 1310720 | tf_op jit(solution)/shard_map/all_gather | solution.py:22
  8.6 178.3 %reduce-scatter.5.cloned.1.call-start = ((), (), s32[]{:S(2)}) async-start(), calls=%async_computation.5 | async-start | bytes 8257536 | tf_op jit(solution)/shard_map/reduce_scatter | solution.py:44
  29.0 4.8 %copy-start = (bf16[128,4096]{1,0:T(8,128)(2,1)S(1)}, bf16[128,4096]{1,0:T(8,128)(2,1)}, u32[]{:S(2)}) copy-start(bf16[128,4096]{1,0:T(8,128)(2,1)} %all-gather.5.cloned.1.call-done) | copy-start | bytes 3145732
  47.3 6.5 %copy-start.1 = (bf16[128,4096]{1,0:T(8,128)(2,1)S(1)}, bf16[128,4096]{1,0:T(8,128)(2,1)}, u32[]{:S(2)}) copy-start(bf16[128,4096]{1,0:T(8,128)(2,1)} %all-gather.3.cloned.1.call-done) | copy-start | bytes 3145732
  53.7 160.2 %reduce-scatter.3.cloned.1.call-start = ((), (), s32[]{:S(2)}) async-start(), calls=%async_computation.4 | async-start | bytes 1310720 | tf_op jit(solution)/shard_map/reduce_scatter | solution.py:37
  53.8 12.0 %slice-start = ((s8[7340032]{0:T(1024)(128)(4,1)}), s8[4194304]{0:T(1024)(128)(4,1)S(1)}, s32[]{:S(2)}) async-start(s8[7340032]{0:T(1024)(128)(4,1)} %bitcast.9), calls=%async_computation.6 | async-start | bytes 8388608
  59.5 6.4 %slice-start.1 = ((s8[7340032]{0:T(1024)(128)(4,1)}), s8[3145728]{0:T(1024)(128)(4,1)S(1)}, s32[]{:S(2)}) async-start(s8[7340032]{0:T(1024)(128)(4,1)} %bitcast.9), calls=%async_computation.7 | async-start | bytes 6291456
Sparse Core Ops, SparseCore 0:
  9.6 19.4 all-gather.4
  30.6 16.7 all-gather.2
  53.9 133.0 reduce-scatter.4
  189.9 23.9 reduce-scatter.2
where the time goes:
time: 221 us; the launch traced here: 220 us
  waiting for transfers between devices  173 us (78%)
  matrix products  31 us (14%)
  between operations  13.8 us (6%)
  other arithmetic  2.66 us (1%)
    reduce_scatter x1, waiting for transfers between devices, body(): lax.psum_scatter(partial_grad.astype(jnp.bfloat16), 'dp', scatter_dimensi...  118 us
    reduce_scatter x1, waiting for transfers between devices, body(): lax.psum_scatter((contract_cols(grad_gate, w_gate) + contract_cols(grad_u...  24.3 us
    all_gather x1, waiting for transfers between devices, body(): lax.all_gather(tokens, 'tensor', axis=0, tiled=True)  20.3 us
    dot_general x3, matrix products, contract_cols(): lax.dot_general(left, right, (((1,), (1,)), ((), ())), preferred_element_...  15.5 us
    all_gather x1, waiting for transfers between devices, body(): lax.all_gather(upstream_grad, 'tensor', axis=0, tiled=True)  9.11 us
    dot_general x1, matrix products, contract_rows(): lax.dot_general(left, right, (((0,), (0,)), ((), ())), preferred_element_...  6.38 us
    dot_general x1, matrix products, body(): gate_pre = jnp.dot(gathered, w_gate, preferred_element_type=jnp.float32)  4.75 us
    dot_general x1, matrix products, body(): up_pre = jnp.dot(gathered, w_up, preferred_element_type=jnp.float32)  4.43 us
  transfers between devices with their start and end apart: 4, of which 4 were waited for; matrix products, arithmetic and copies ran while one was open for 12% of the time, Pallas kernels for 0%

commit v1 on v0

v1 whole, which is shorter than its diff:
```python
import functools

import jax
import jax.numpy as jnp
from jax import lax
from jax.experimental import pallas as pl
from jax.experimental.pallas import tpu as pltpu
from jax.sharding import PartitionSpec as P


def contract_rows(left, right):
    return lax.dot_general(
        left, right, (((0,), (0,)), ((), ())), preferred_element_type=jnp.float32
    )


def contract_cols(left, right):
    return lax.dot_general(
        left, right, (((1,), (1,)), ((), ())), preferred_element_type=jnp.float32
    )


def plain_body(tokens, upstream_grad, w_gate, w_up, w_down):
    n_dp = lax.axis_size("dp")
    rows, width = upstream_grad.shape
    gathered = lax.all_gather(tokens, "tensor", axis=0, tiled=True)
    upstream = lax.all_gather(upstream_grad, "tensor", axis=0, tiled=True)
    mine = lax.all_to_all(
        upstream_grad.reshape(rows, n_dp, width // n_dp), "dp", split_axis=1, concat_axis=0
    )
    mine = lax.all_gather(mine.reshape(n_dp, rows, width // n_dp), "tensor", axis=1, tiled=True)
    mine = mine.reshape(-1, width // n_dp)
    gate_pre = jnp.dot(gathered, w_gate, preferred_element_type=jnp.float32)
    up_pre = jnp.dot(gathered, w_up, preferred_element_type=jnp.float32)
    sig_gate = jax.nn.sigmoid(gate_pre)
    act_gate = gate_pre * sig_gate
    hidden = (act_gate * up_pre).astype(jnp.bfloat16)
    hidden_all = lax.all_gather(hidden, "dp", axis=0, tiled=True)
    grad_hidden = contract_cols(upstream, w_down).astype(jnp.bfloat16)
    hidden_f = grad_hidden.astype(jnp.float32)
    grad_gate = (hidden_f * up_pre * sig_gate * (1.0 + gate_pre * (1.0 - sig_gate))).astype(
        jnp.bfloat16
    )
    grad_up = (hidden_f * act_gate).astype(jnp.bfloat16)
    factor = float(hidden_all.shape[0]) ** (-0.5)
    summed = lax.psum_scatter(
        (contract_cols(grad_gate, w_gate) + contract_cols(grad_up, w_up)).astype(jnp.bfloat16),
        "tensor",
        scatter_dimension=0,
        tiled=True,
    )
    grad_down = contract_rows(hidden_all, mine) * factor
    return (summed, grad_down)


MESH = pl.DeviceIdType.MESH
BF16 = jnp.bfloat16
F32 = jnp.float32
PARTS = 4
UNITS = 256


def kernel(
    n_dp, n_tensor,
    tok, upg, wg_h, wu_h, wd_h,
    gtok_h, gdown_h,
    wg, wu, wd, gt, gu, gate, up, gh, gboth, hid, upc, part, pc_out, pc_in, cs_out, cs_in,
    gtok, gdown,
    w_sem, loc_sem, out_sem,
    core_s, core_r, x_s, x_r, fwd_s, fwd_r,
    a2a_s, a2a_r, uc_s, uc_r, ux_s, ux_r, uf_s, uf_r,
    hy_s, hy_r, hz_s, hz_r, hf_s, hf_r,
    pc_s, pc_r, cs_s, cs_r,
):
    rows, width = tok.shape
    units = wg_h.shape[1]
    replica = rows * n_tensor
    step = width // PARTS
    mine = width // n_dp
    n_x, n_z = n_tensor // 2, n_dp // 2
    d, t = lax.axis_index("dp"), lax.axis_index("tensor")
    c, x = lax.rem(t, 2), lax.div(t, 2)
    y, z = lax.rem(d, 2), lax.div(d, 2)
    core = (d, x * 2 + 1 - c)
    ypeer = (z * 2 + 1 - y, t)
    xs, zs = range(1, n_x), range(1, n_z)
    pieces = [(f, min(UNITS, units - f)) for f in range(0, units, UNITS)]

    def x_to(o):
        return (d, lax.rem(x + o, n_x) * 2 + c)

    def x_from(o):
        return lax.rem(x + n_x - o, n_x) * 2 + c

    def z_to(o):
        return (lax.rem(z + o, n_z) * 2 + y, t)

    def z_from(o):
        return lax.rem(z + n_z - o, n_z) * 2 + y

    def dp_to(o):
        return lax.rem(d + o, n_dp)

    def of_tensor(i):
        return pl.ds(pl.multiple_of(i * rows, rows), rows)

    def of_dp(i):
        return pl.ds(pl.multiple_of(i * replica, replica), replica)

    def cut(k):
        return pl.ds(k * step, step)

    def remote(src, dst, s, r, to):
        return pltpu.make_async_remote_copy(
            src_ref=src, dst_ref=dst, send_sem=s, recv_sem=r, device_id=to, device_id_type=MESH
        )

    loads = [[
        pltpu.make_async_copy(wg_h.at[cut(k), :], wg.at[cut(k), :], w_sem.at[0, k]),
        pltpu.make_async_copy(wu_h.at[cut(k), :], wu.at[cut(k), :], w_sem.at[1, k]),
        pltpu.make_async_copy(wd_h.at[:, cut(k)], wd.at[:, cut(k)], w_sem.at[2, k]),
    ] for k in range(PARTS)]
    own = [
        pltpu.make_async_copy(tok, gt.at[of_tensor(t), :], loc_sem.at[0]),
        pltpu.make_async_copy(upg, gu.at[of_tensor(t), :], loc_sem.at[1]),
        pltpu.make_async_copy(
            upg.at[:, pl.ds(pl.multiple_of(d * mine, mine), mine)],
            upc.at[d, of_tensor(t), :], loc_sem.at[2]),
    ]
    for copy in own:
        copy.start()
    for k in range(PARTS):
        loads[k][0].start()
        loads[k][1].start()

    barrier = pltpu.get_barrier_semaphore()
    pl.semaphore_signal(barrier, inc=1, device_id=core, device_id_type=MESH)
    for o in xs:
        pl.semaphore_signal(barrier, inc=1, device_id=x_to(o), device_id_type=MESH)
    for o in range(1, n_dp):
        pl.semaphore_signal(barrier, inc=1, device_id=(dp_to(o), t), device_id_type=MESH)
    pl.semaphore_wait(barrier, 1 + (n_x - 1) + (n_dp - 1))

    to_core, to_x, passed = {}, {}, {}
    for a, (src, dst) in enumerate(((tok, gt), (upg, gu))):
        for k in range(PARTS):
            to_core[a, k] = remote(
                src.at[:, cut(k)], dst.at[of_tensor(t), cut(k)],
                core_s.at[a, k], core_r.at[a, k], core)
            for o in xs:
                to_x[a, k, o] = remote(
                    src.at[:, cut(k)], dst.at[of_tensor(t), cut(k)],
                    x_s.at[a, k, o - 1], x_r.at[a, k, o - 1], x_to(o))
                there = dst.at[of_tensor(x_from(o)), cut(k)]
                passed[a, k, o] = remote(
                    there, there, fwd_s.at[a, k, o - 1], fwd_r.at[a, k, o - 1], core)
    for k in range(PARTS):
        for o in xs:
            to_x[0, k, o].start()
        to_core[0, k].start()
    exchange = [
        remote(
            upg.at[:, pl.ds(pl.multiple_of(dp_to(o) * mine, mine), mine)],
            upc.at[d, of_tensor(t), :],
            a2a_s.at[o - 1], a2a_r.at[o - 1], (dp_to(o), t))
        for o in range(1, n_dp)
    ]
    for copy in exchange:
        copy.start()
    for k in range(PARTS):
        to_core[1, k].start()

    def arrive(a, k):
        for o in xs:
            to_x[a, k, o].wait_recv()
            passed[a, k, o].start()

    def complete(a, k):
        to_core[a, k].wait_recv()
        for o in xs:
            passed[a, k, o].wait_recv()

    hid_y, hid_z, hid_f = {}, {}, {}
    for j, (f, n) in enumerate(pieces):
        here = hid.at[pl.ds(f, n), of_dp(d)]
        hid_y[j] = remote(here, here, hy_s.at[j], hy_r.at[j], ypeer)
        for o in zs:
            hid_z[j, o] = remote(here, here, hz_s.at[j, o - 1], hz_r.at[j, o - 1], z_to(o))
            there = hid.at[pl.ds(f, n), of_dp(z_from(o))]
            hid_f[j, o] = remote(there, there, hf_s.at[j, o - 1], hf_r.at[j, o - 1], ypeer)

    def pass_hidden(j):
        for o in zs:
            hid_z[j, o].wait_recv()
            hid_f[j, o].start()

    own[0].wait()
    for k in range(PARTS):
        arrive(0, k)
        for o in xs:
            to_x[1, k, o].start()
        loads[k][2].start()
        complete(0, k)
        loads[k][0].wait()
        loads[k][1].wait()
        lhs = gt[:, k * step:(k + 1) * step]
        for j, (f, n) in enumerate(pieces):
            fs, ks = slice(f, f + n), slice(k * step, (k + 1) * step)
            g = jnp.dot(lhs, wg[ks, fs], preferred_element_type=F32)
            u = jnp.dot(lhs, wu[ks, fs], preferred_element_type=F32)
            if k > 0:
                g, u = gate[:, fs] + g, up[:, fs] + u
            gate[:, fs] = g
            up[:, fs] = u
            if k == PARTS - 1:
                h = g * jax.nn.sigmoid(g) * u
                hid[fs, of_dp(d)] = h.T.astype(BF16)
                for o in zs:
                    hid_z[j, o].start()
                hid_y[j].start()

    own[2].wait()
    for copy in exchange:
        copy.wait_recv()
    block = upc.at[:, of_tensor(t), :]
    up_core = remote(block, block, uc_s, uc_r, core)
    up_core.start()
    up_x, up_f = {}, {}
    for o in xs:
        up_x[o] = remote(block, block, ux_s.at[o - 1], ux_r.at[o - 1], x_to(o))
        there = upc.at[:, of_tensor(x_from(o)), :]
        up_f[o] = remote(there, there, uf_s.at[o - 1], uf_r.at[o - 1], core)

    own[1].wait()
    for k in range(PARTS):
        arrive(1, k)
        complete(1, k)
        loads[k][2].wait()
        ks = slice(k * step, (k + 1) * step)
        lhs = gu[:, ks]
        for f, n in pieces:
            fs = slice(f, f + n)
            p = contract_cols(lhs, wd[fs, ks])
            if k > 0:
                p = gh[:, fs] + p
            gh[:, fs] = p
    for o in xs:
        up_x[o].start()
    for f, n in pieces:
        fs = slice(f, f + n)
        g, u = gate[:, fs], up[:, fs]
        h = gh[:, fs].astype(BF16).astype(F32)
        sig = jax.nn.sigmoid(g)
        gboth[:, fs] = (h * u * sig * (1.0 + g * (1.0 - sig))).astype(BF16)
        gboth[:, units + f:units + f + n] = (h * (g * sig)).astype(BF16)
    pass_hidden(0)

    swap, chip = {}, {}
    for q in range(PARTS):
        swap[q] = remote(
            pc_out.at[:, :, cut(q)], pc_in.at[:, :, cut(q)], pc_s.at[q], pc_r.at[q], core)
        for o in xs:
            chip[q, o] = remote(
                cs_out.at[o - 1, :, cut(q)], cs_in.at[o - 1, :, cut(q)],
                cs_s.at[q, o - 1], cs_r.at[q, o - 1], x_to(o))

    def add_cores(q):
        swap[q].wait_recv()
        qs = slice(q * step, (q + 1) * step)
        for o in xs:
            to = lax.rem(x + o, n_x)
            both = part[of_tensor(to * 2 + c), qs] + pc_in[to, :, qs].astype(F32)
            cs_out[o - 1, :, qs] = both.astype(BF16)
            chip[q, o].start()

    for q in range(PARTS):
        qs = slice(q * step, (q + 1) * step)
        part[:, qs] = contract_cols(gboth[:, :units], wg[qs, :]) + contract_cols(
            gboth[:, units:], wu[qs, :])
        for i in range(n_x):
            pc_out[i, :, qs] = part[of_tensor(i * 2 + 1 - c), qs].astype(BF16)
        swap[q].start()
        if q > 0:
            add_cores(q - 1)
    add_cores(PARTS - 1)
    pass_hidden(1)
    for o in xs:
        up_x[o].wait_recv()
        up_f[o].start()
    for q in range(PARTS):
        qs = slice(q * step, (q + 1) * step)
        total = part[of_tensor(t), qs] + pc_in[x, :, qs].astype(F32)
        for o in xs:
            chip[q, o].wait_recv()
            total = total + cs_in[o - 1, :, qs].astype(F32)
        gtok[:, qs] = total.astype(BF16)
    results = [pltpu.make_async_copy(gtok, gtok_h, out_sem.at[len(pieces)])]
    results[0].start()

    up_core.wait_recv()
    for o in xs:
        up_f[o].wait_recv()
    factor = float(n_dp * replica) ** (-0.5)
    for j, (f, n) in enumerate(pieces):
        if j + 2 < len(pieces):
            pass_hidden(j + 2)
        hid_y[j].wait_recv()
        for o in zs:
            hid_f[j, o].wait_recv()
        fs = slice(f, f + n)
        gdown[fs, :] = jnp.dot(
            hid[fs, :], upc[...].reshape(n_dp * replica, mine), preferred_element_type=F32
        ) * factor
        copy = pltpu.make_async_copy(
            gdown.at[pl.ds(f, n), :], gdown_h.at[pl.ds(f, n), :], out_sem.at[j])
        copy.start()
        results.append(copy)

    sent = [*to_core.values(), *to_x.values(), *passed.values(), *exchange, up_core,
            *up_x.values(), *up_f.values(), *hid_y.values(), *hid_z.values(), *hid_f.values(),
            *swap.values(), *chip.values()]
    for copy in sent:
        copy.wait_send()
    for copy in results:
        copy.wait()


def body(tokens, upstream_grad, w_gate, w_up, w_down):
    n_dp, n_tensor = lax.axis_size("dp"), lax.axis_size("tensor")
    rows, width = tokens.shape
    units = w_gate.shape[1]
    mine = width // n_dp
    n_x, n_z = n_tensor // 2, n_dp // 2
    if rows % 16 or n_tensor % 2 or n_dp % 2 or n_x < 2 or n_z < 2:
        return plain_body(tokens, upstream_grad, w_gate, w_up, w_down)
    replica = rows * n_tensor
    n_pieces = -(-units // UNITS)
    dma = pltpu.SemaphoreType.DMA
    vmem = pltpu.VMEM

    def pair(*shape):
        return [dma(shape), dma(shape)] if shape else [dma, dma]

    scratch = [
        vmem((width, units), BF16), vmem((width, units), BF16), vmem((units, width), BF16),
        vmem((replica, width), BF16), vmem((replica, width), BF16),
        vmem((replica, units), F32), vmem((replica, units), F32), vmem((replica, units), F32),
        vmem((replica, 2 * units), BF16),
        vmem((units, n_dp * replica), BF16),
        vmem((n_dp, replica, mine), BF16),
        vmem((replica, width), F32),
        vmem((n_x, rows, width), BF16), vmem((n_x, rows, width), BF16),
        vmem((n_x - 1, rows, width), BF16), vmem((n_x - 1, rows, width), BF16),
        vmem((rows, width), BF16), vmem((units, mine), F32),
        dma((3, PARTS)), dma((3,)), dma((n_pieces + 1,)),
        *pair(2, PARTS), *pair(2, PARTS, n_x - 1), *pair(2, PARTS, n_x - 1),
        *pair(n_dp - 1), *pair(), *pair(n_x - 1), *pair(n_x - 1),
        *pair(n_pieces), *pair(n_pieces, n_z - 1), *pair(n_pieces, n_z - 1),
        *pair(PARTS), *pair(PARTS, n_x - 1),
    ]
    return pl.pallas_call(
        functools.partial(kernel, n_dp, n_tensor),
        out_shape=(
            jax.ShapeDtypeStruct((rows, width), BF16),
            jax.ShapeDtypeStruct((units, mine), F32),
        ),
        in_specs=[pl.BlockSpec(memory_space=pl.ANY)] * 5,
        out_specs=(pl.BlockSpec(memory_space=pl.ANY),) * 2,
        scratch_shapes=scratch,
        compiler_params=pltpu.CompilerParams(
            collective_id=0, has_side_effects=True, vmem_limit_bytes=56 * 1024 * 1024
        ),
        cost_estimate=pl.CostEstimate(
            flops=2 * replica * width * units * 6, bytes_accessed=6 * width * units,
            transcendentals=replica * units,
        ),
    )(tokens, upstream_grad, w_gate, w_up, w_down)


def solution(mesh):
    in_specs = (
        P(("dp", "tensor"), None),
        P(("dp", "tensor"), None),
        P(None, "tensor"),
        P(None, "tensor"),
        P("tensor", None),
    )
    out_specs = (P(("dp", "tensor"), None), P("tensor", "dp"))
    return jax.shard_map(body, mesh=mesh, in_specs=in_specs, out_specs=out_specs, check_vma=False)
```

time: 221 us -> 54.5 us (0.25)
  the two profiles are of different devices: /device:TPU:0 before, /device:TPU:13 now
where the time goes in v1:
time: 54.5 us; the launch traced here: 54.3 us
  Pallas kernels  49.1 us (90%)
  local copies, waits for them, and re-layouts  4.54 us (8%)
  between operations  0.64 us (1%)
    pallas_call x1, Pallas kernels, body(): pl.pallas_call(functools.partial(kernel, n_dp, n_tensor), out_shape=(jax....  49.1 us
    unnamed x2, local copies, waits for them, and re-layouts  4.54 us

profile of v1, /device:TPU:13, one launch (start us, length us, event | category | flops | bytes accessed | tf_op | source)
XLA Modules:
  0.0 54.3 jit_solution(3464486884255909906)
XLA Ops:
  0.6 49.1 %shard_map.68 = (bf16[32,4096]{1,0:T(8,128)(2,1)}, f32[896,512]{1,0:T(8,128)}) custom-call(bf16[32,4096]{1,0:T(8,128)(2,1)} %tok.1, bf16[32,4096]{1,0:T(8,128)(2,1)} %upg.1, bf16[4096,896]{1,0:T(8,128)(2,1)} %wg_h.1, bf16[4096,896]{1,0:T(8,128)(2,1)} %wu_h.1, bf16[896,4096]{1,0:T(8,128)(2,1)} %wd_h.1), custom_call_target="tpu_custom_call" | custom-call | flops 5637144576 | bytes 22020096 | tf_op jit(solution)/shard_map/pallas_call | solution.py:361
  49.8 1.7 %copy.9 = bf16[32,4096]{1,0:T(8,128)(2,1)} copy(bf16[32,4096]{1,0:T(8,128)(2,1)} %get-tuple-element.4) | data formatting | bytes 524288
  51.4 2.9 %copy.10 = f32[896,512]{1,0:T(8,128)} copy(f32[896,512]{1,0:T(8,128)} %get-tuple-element.5) | data formatting | bytes 3670016

commit v2 on v1

--- a/solution.py
+++ b/solution.py
@@ -104,8 +104,8 @@
     def of_tensor(i):
         return pl.ds(pl.multiple_of(i * rows, rows), rows)
 
-    def of_dp(i):
-        return pl.ds(pl.multiple_of(i * replica, replica), replica)
+    def of_chip(o):
+        return pl.ds(pl.multiple_of(lax.rem(x + n_x - o, n_x) * 2 * rows, 2 * rows), 2 * rows)
 
     def cut(k):
         return pl.ds(k * step, step)
@@ -129,7 +129,7 @@
     ]
     for copy in own:
         copy.start()
-    for k in range(PARTS):
+    for k in range(2):
         loads[k][0].start()
         loads[k][1].start()
 
@@ -181,43 +181,55 @@
             passed[a, k, o].wait_recv()
 
     hid_y, hid_z, hid_f = {}, {}, {}
-    for j, (f, n) in enumerate(pieces):
-        here = hid.at[pl.ds(f, n), of_dp(d)]
-        hid_y[j] = remote(here, here, hy_s.at[j], hy_r.at[j], ypeer)
+    for s in range(n_x):
+        for j in range(len(pieces)):
+            here = hid[j].at[d, of_chip(s), :]
+            hid_y[s, j] = remote(here, here, hy_s.at[s, j], hy_r.at[s, j], ypeer)
+            for o in zs:
+                hid_z[s, j, o] = remote(
+                    here, here, hz_s.at[s, j, o - 1], hz_r.at[s, j, o - 1], z_to(o))
+                there = hid[j].at[z_from(o), of_chip(s), :]
+                hid_f[s, j, o] = remote(
+                    there, there, hf_s.at[s, j, o - 1], hf_r.at[s, j, o - 1], ypeer)
+
+    def pass_hidden(s, j):
         for o in zs:
-            hid_z[j, o] = remote(here, here, hz_s.at[j, o - 1], hz_r.at[j, o - 1], z_to(o))
-            there = hid.at[pl.ds(f, n), of_dp(z_from(o))]
-            hid_f[j, o] = remote(there, there, hf_s.at[j, o - 1], hf_r.at[j, o - 1], ypeer)
-
-    def pass_hidden(j):
-        for o in zs:
-            hid_z[j, o].wait_recv()
-            hid_f[j, o].start()
-
-    own[0].wait()
-    for k in range(PARTS):
-        arrive(0, k)
-        for o in xs:
-            to_x[1, k, o].start()
-        loads[k][2].start()
-        complete(0, k)
-        loads[k][0].wait()
-        loads[k][1].wait()
-        lhs = gt[:, k * step:(k + 1) * step]
+            hid_z[s, j, o].wait_recv()
+            hid_f[s, j, o].start()
+
+    def forward(s, k):
+        lhs = gt[of_chip(s), k * step:(k + 1) * step]
         for j, (f, n) in enumerate(pieces):
             fs, ks = slice(f, f + n), slice(k * step, (k + 1) * step)
             g = jnp.dot(lhs, wg[ks, fs], preferred_element_type=F32)
             u = jnp.dot(lhs, wu[ks, fs], preferred_element_type=F32)
             if k > 0:
-                g, u = gate[:, fs] + g, up[:, fs] + u
-            gate[:, fs] = g
-            up[:, fs] = u
+                g, u = gate[of_chip(s), fs] + g, up[of_chip(s), fs] + u
+            gate[of_chip(s), fs] = g
+            up[of_chip(s), fs] = u
             if k == PARTS - 1:
-                h = g * jax.nn.sigmoid(g) * u
-                hid[fs, of_dp(d)] = h.T.astype(BF16)
+                hid[j][d, of_chip(s), :] = (g * jax.nn.sigmoid(g) * u).astype(BF16)
                 for o in zs:
-                    hid_z[j, o].start()
-                hid_y[j].start()
+                    hid_z[s, j, o].start()
+                hid_y[s, j].start()
+
+    own[0].wait()
+    for k in range(PARTS):
+        to_core[0, k].wait_recv()
+        loads[k][0].wait()
+        loads[k][1].wait()
+        if k + 2 < PARTS:
+            loads[k + 2][0].start()
+            loads[k + 2][1].start()
+        forward(0, k)
+    for k in range(PARTS):
+        arrive(0, k)
+        for o in xs:
+            to_x[1, k, o].start()
+        loads[k][2].start()
+        for o in xs:
+            passed[0, k, o].wait_recv()
+            forward(o, k)
 
     own[2].wait()
     for copy in exchange:
@@ -244,6 +256,7 @@
             if k > 0:
                 p = gh[:, fs] + p
             gh[:, fs] = p
+        pass_hidden(0, k)
     for o in xs:
         up_x[o].start()
     for f, n in pieces:
@@ -253,7 +266,6 @@
         sig = jax.nn.sigmoid(g)
         gboth[:, fs] = (h * u * sig * (1.0 + g * (1.0 - sig))).astype(BF16)
         gboth[:, units + f:units + f + n] = (h * (g * sig)).astype(BF16)
-    pass_hidden(0)
 
     swap, chip = {}, {}
     for q in range(PARTS):
@@ -282,8 +294,10 @@
         swap[q].start()
         if q > 0:
             add_cores(q - 1)
+        if q == 2:
+            pass_hidden(1, 0)
     add_cores(PARTS - 1)
-    pass_hidden(1)
+    pass_hidden(1, 1)
     for o in xs:
         up_x[o].wait_recv()
         up_f[o].start()
@@ -301,15 +315,21 @@
     for o in xs:
         up_f[o].wait_recv()
     factor = float(n_dp * replica) ** (-0.5)
+    pending = [(s, j) for s in range(n_x) for j in range(len(pieces))]
+    pending = [p for p in pending if p not in ((0, 0), (0, 1), (0, 2), (0, 3), (1, 0), (1, 1))]
+    for p in pending[:1]:
+        pass_hidden(*p)
     for j, (f, n) in enumerate(pieces):
-        if j + 2 < len(pieces):
-            pass_hidden(j + 2)
-        hid_y[j].wait_recv()
-        for o in zs:
-            hid_f[j, o].wait_recv()
+        if j == 1:
+            for p in pending[1:]:
+                pass_hidden(*p)
+        for s in range(n_x):
+            hid_y[s, j].wait_recv()
+            for o in zs:
+                hid_f[s, j, o].wait_recv()
         fs = slice(f, f + n)
-        gdown[fs, :] = jnp.dot(
-            hid[fs, :], upc[...].reshape(n_dp * replica, mine), preferred_element_type=F32
+        gdown[fs, :] = contract_rows(
+            hid[j][...].reshape(n_dp * replica, n), upc[...].reshape(n_dp * replica, mine)
         ) * factor
         copy = pltpu.make_async_copy(
             gdown.at[pl.ds(f, n), :], gdown_h.at[pl.ds(f, n), :], out_sem.at[j])
@@ -325,13 +345,28 @@
         copy.wait()
 
 
+PLACED = 8
+
+
+def place(tokens_in, down_in, tokens_out, down_out, sem):
+    part = down_in.shape[0] // PLACED
+    copies = [pltpu.make_async_copy(tokens_in, tokens_out, sem.at[PLACED])]
+    for i in range(PLACED):
+        at = pl.ds(i * part, part)
+        copies.append(pltpu.make_async_copy(down_in.at[at, :], down_out.at[at, :], sem.at[i]))
+    for copy in copies:
+        copy.start()
+    for copy in copies:
+        copy.wait()
+
+
 def body(tokens, upstream_grad, w_gate, w_up, w_down):
     n_dp, n_tensor = lax.axis_size("dp"), lax.axis_size("tensor")
     rows, width = tokens.shape
     units = w_gate.shape[1]
     mine = width // n_dp
     n_x, n_z = n_tensor // 2, n_dp // 2
-    if rows % 16 or n_tensor % 2 or n_dp % 2 or n_x < 2 or n_z < 2:
+    if rows % 16 or n_tensor % 2 or n_dp % 2 or n_x != 2 or n_z < 2 or len(range(0, units, UNITS)) != PARTS:
         return plain_body(tokens, upstream_grad, w_gate, w_up, w_down)
     replica = rows * n_tensor
     n_pieces = -(-units // UNITS)
@@ -346,7 +381,7 @@
         vmem((replica, width), BF16), vmem((replica, width), BF16),
         vmem((replica, units), F32), vmem((replica, units), F32), vmem((replica, units), F32),
         vmem((replica, 2 * units), BF16),
-        vmem((units, n_dp * replica), BF16),
+        [vmem((n_dp, replica, min(UNITS, units - f)), BF16) for f in range(0, units, UNITS)],
         vmem((n_dp, replica, mine), BF16),
         vmem((replica, width), F32),
         vmem((n_x, rows, width), BF16), vmem((n_x, rows, width), BF16),
@@ -355,10 +390,10 @@
         dma((3, PARTS)), dma((3,)), dma((n_pieces + 1,)),
         *pair(2, PARTS), *pair(2, PARTS, n_x - 1), *pair(2, PARTS, n_x - 1),
         *pair(n_dp - 1), *pair(), *pair(n_x - 1), *pair(n_x - 1),
-        *pair(n_pieces), *pair(n_pieces, n_z - 1), *pair(n_pieces, n_z - 1),
+        *pair(n_x, n_pieces), *pair(n_x, n_pieces, n_z - 1), *pair(n_x, n_pieces, n_z - 1),
         *pair(PARTS), *pair(PARTS, n_x - 1),
     ]
-    return pl.pallas_call(
+    grads = pl.pallas_call(
         functools.partial(kernel, n_dp, n_tensor),
         out_shape=(
             jax.ShapeDtypeStruct((rows, width), BF16),
@@ -375,6 +410,13 @@
             transcendentals=replica * units,
         ),
     )(tokens, upstream_grad, w_gate, w_up, w_down)
+    return pl.pallas_call(
+        place,
+        out_shape=tuple(jax.ShapeDtypeStruct(g.shape, g.dtype) for g in grads),
+        in_specs=[pl.BlockSpec(memory_space=pltpu.HBM)] * 2,
+        out_specs=(pl.BlockSpec(memory_space=pltpu.HBM),) * 2,
+        scratch_shapes=[dma((PLACED + 1,))],
+    )(*grads)
 
 
 def solution(mesh):

time: 54.5 us -> 113 us (2.07)
  the two profiles are of different devices: /device:TPU:13 before, /device:TPU:0 now
where the time goes in v2:
time: 113 us
  Pallas kernels  112 us (99%)
    pallas_call x1, Pallas kernels, body(): pl.pallas_call(place, out_shape=tuple((jax.ShapeDtypeStruct(g.shape, g.dt...  64.7 us
    pallas_call x1, Pallas kernels, body(): pl.pallas_call(functools.partial(kernel, n_dp, n_tensor), out_shape=(jax....  47.4 us

profile of v2, /device:TPU:0, one launch (start us, length us, event | category | flops | bytes accessed | tf_op | source)
XLA Modules:
  0.0 112.8 jit_solution(13196877891801835434)
XLA Ops:
  0.6 47.4 %shard_map.68 = (bf16[32,4096]{1,0:T(8,128)(2,1)}, f32[896,512]{1,0:T(8,128)}) custom-call(bf16[32,4096]{1,0:T(8,128)(2,1)} %tok.1, bf16[32,4096]{1,0:T(8,128)(2,1)} %upg.1, bf16[4096,896]{1,0:T(8,128)(2,1)} %wg_h.1, bf16[4096,896]{1,0:T(8,128)(2,1)} %wu_h.1, bf16[896,4096]{1,0:T(8,128)(2,1)} %wd_h.1), custom_call_target="tpu_custom_call" | custom-call | flops 5637144576 | bytes 22020096 | tf_op jit(solution)/shard_map/pallas_call | solution.py:396
  48.1 64.7 %shard_map.69 = (bf16[32,4096]{1,0:T(8,128)(2,1)}, f32[896,512]{1,0:T(8,128)}) custom-call(bf16[32,4096]{1,0:T(8,128)(2,1)} %get-tuple-element.4.tokens_in, f32[896,512]{1,0:T(8,128)} %get-tuple-element.5.down_in), custom_call_target="tpu_custom_call" | custom-call | tf_op jit(solution)/shard_map/pallas_call | solution.py:413

commit v3 on v2

--- a/solution.py
+++ b/solution.py
@@ -140,18 +140,21 @@
     for o in range(1, n_dp):
         pl.semaphore_signal(barrier, inc=1, device_id=(dp_to(o), t), device_id_type=MESH)
     pl.semaphore_wait(barrier, 1 + (n_x - 1) + (n_dp - 1))
+    own[0].wait()
+    own[1].wait()
 
     to_core, to_x, passed = {}, {}, {}
-    for a, (src, dst) in enumerate(((tok, gt), (upg, gu))):
+    for a, all_rows in enumerate((gt, gu)):
         for k in range(PARTS):
+            here = all_rows.at[of_tensor(t), cut(k)]
             to_core[a, k] = remote(
-                src.at[:, cut(k)], dst.at[of_tensor(t), cut(k)],
+                here, here,
                 core_s.at[a, k], core_r.at[a, k], core)
             for o in xs:
                 to_x[a, k, o] = remote(
-                    src.at[:, cut(k)], dst.at[of_tensor(t), cut(k)],
+                    here, here,
                     x_s.at[a, k, o - 1], x_r.at[a, k, o - 1], x_to(o))
-                there = dst.at[of_tensor(x_from(o)), cut(k)]
+                there = all_rows.at[of_tensor(x_from(o)), cut(k)]
                 passed[a, k, o] = remote(
                     there, there, fwd_s.at[a, k, o - 1], fwd_r.at[a, k, o - 1], core)
     for k in range(PARTS):
@@ -160,7 +163,7 @@
         to_core[0, k].start()
     exchange = [
         remote(
-            upg.at[:, pl.ds(pl.multiple_of(dp_to(o) * mine, mine), mine)],
+            gu.at[of_tensor(t), pl.ds(pl.multiple_of(dp_to(o) * mine, mine), mine)],
             upc.at[d, of_tensor(t), :],
             a2a_s.at[o - 1], a2a_r.at[o - 1], (dp_to(o), t))
         for o in range(1, n_dp)
@@ -213,7 +216,6 @@
                     hid_z[s, j, o].start()
                 hid_y[s, j].start()
 
-    own[0].wait()
     for k in range(PARTS):
         to_core[0, k].wait_recv()
         loads[k][0].wait()
@@ -243,7 +245,6 @@
         there = upc.at[:, of_tensor(x_from(o)), :]
         up_f[o] = remote(there, there, uf_s.at[o - 1], uf_r.at[o - 1], core)
 
-    own[1].wait()
     for k in range(PARTS):
         arrive(1, k)
         complete(1, k)
@@ -252,17 +253,17 @@
         lhs = gu[:, ks]
         for f, n in pieces:
             fs = slice(f, f + n)
-            p = contract_cols(lhs, wd[fs, ks])
+            p = contract_cols(wd[fs, ks], lhs)
             if k > 0:
-                p = gh[:, fs] + p
-            gh[:, fs] = p
+                p = gh[fs, :] + p
+            gh[fs, :] = p
         pass_hidden(0, k)
     for o in xs:
         up_x[o].start()
     for f, n in pieces:
         fs = slice(f, f + n)
         g, u = gate[:, fs], up[:, fs]
-        h = gh[:, fs].astype(BF16).astype(F32)
+        h = gh[fs, :].T.astype(BF16).astype(F32)
         sig = jax.nn.sigmoid(g)
         gboth[:, fs] = (h * u * sig * (1.0 + g * (1.0 - sig))).astype(BF16)
         gboth[:, units + f:units + f + n] = (h * (g * sig)).astype(BF16)
@@ -287,8 +288,9 @@
 
     for q in range(PARTS):
         qs = slice(q * step, (q + 1) * step)
-        part[:, qs] = contract_cols(gboth[:, :units], wg[qs, :]) + contract_cols(
-            gboth[:, units:], wu[qs, :])
+        both = contract_cols(wg[qs, :], gboth[:, :units]) + contract_cols(
+            wu[qs, :], gboth[:, units:])
+        part[:, qs] = both.T
         for i in range(n_x):
             pc_out[i, :, qs] = part[of_tensor(i * 2 + 1 - c), qs].astype(BF16)
         swap[q].start()
@@ -345,18 +347,23 @@
         copy.wait()
 
 
-PLACED = 8
-
-
-def place(tokens_in, down_in, tokens_out, down_out, sem):
-    part = down_in.shape[0] // PLACED
-    copies = [pltpu.make_async_copy(tokens_in, tokens_out, sem.at[PLACED])]
+PLACED = 4
+
+
+def place(tokens_in, down_in, tokens_out, down_out, tokens_held, down_held, read, written):
+    n = down_in.shape[0] // PLACED
+    moves = [(tokens_in, tokens_held, tokens_out)]
     for i in range(PLACED):
-        at = pl.ds(i * part, part)
-        copies.append(pltpu.make_async_copy(down_in.at[at, :], down_out.at[at, :], sem.at[i]))
-    for copy in copies:
+        at = pl.ds(i * n, n)
+        moves.append((down_in.at[at, :], down_held.at[at, :], down_out.at[at, :]))
+    ins = [pltpu.make_async_copy(a, b, read.at[i]) for i, (a, b, _) in enumerate(moves)]
+    outs = [pltpu.make_async_copy(b, c, written.at[i]) for i, (_, b, c) in enumerate(moves)]
+    for copy in ins:
         copy.start()
-    for copy in copies:
+    for copy, then in zip(ins, outs):
+        copy.wait()
+        then.start()
+    for copy in outs:
         copy.wait()
 
 
@@ -379,7 +386,7 @@
     scratch = [
         vmem((width, units), BF16), vmem((width, units), BF16), vmem((units, width), BF16),
         vmem((replica, width), BF16), vmem((replica, width), BF16),
-        vmem((replica, units), F32), vmem((replica, units), F32), vmem((replica, units), F32),
+        vmem((replica, units), F32), vmem((replica, units), F32), vmem((units, replica), F32),
         vmem((replica, 2 * units), BF16),
         [vmem((n_dp, replica, min(UNITS, units - f)), BF16) for f in range(0, units, UNITS)],
         vmem((n_dp, replica, mine), BF16),
@@ -415,7 +422,10 @@
         out_shape=tuple(jax.ShapeDtypeStruct(g.shape, g.dtype) for g in grads),
         in_specs=[pl.BlockSpec(memory_space=pltpu.HBM)] * 2,
         out_specs=(pl.BlockSpec(memory_space=pltpu.HBM),) * 2,
-        scratch_shapes=[dma((PLACED + 1,))],
+        scratch_shapes=[
+            vmem((rows, width), BF16), vmem((units, mine), F32),
+            dma((PLACED + 1,)), dma((PLACED + 1,)),
+        ],
     )(*grads)
 
 

time: 113 us -> 51.1 us (0.45)
  Pallas kernels: 112 us -> 49.8 us
    pallas_call x1, Pallas kernels: 64.7 us -> 2.41 us  [body(): pl.pallas_call(place, out_shape=tuple((jax.ShapeDtypeStruct(g.shape, g.dt...]
where the time goes in v3:
time: 51.1 us; the launch traced here: 50.4 us
  Pallas kernels  49.8 us (97%)
  between operations  0.64 us (1%)
    pallas_call x1, Pallas kernels, body(): pl.pallas_call(functools.partial(kernel, n_dp, n_tensor), out_shape=(jax....  47.4 us
    pallas_call x1, Pallas kernels, body(): pl.pallas_call(place, out_shape=tuple((jax.ShapeDtypeStruct(g.shape, g.dt...  2.41 us

profile of v3, /device:TPU:0, one launch (start us, length us, event | category | flops | bytes accessed | tf_op | source)
XLA Modules:
  0.0 50.4 jit_solution(14898151632457355536)
XLA Ops:
  0.6 47.4 %shard_map.68 = (bf16[32,4096]{1,0:T(8,128)(2,1)}, f32[896,512]{1,0:T(8,128)}) custom-call(bf16[32,4096]{1,0:T(8,128)(2,1)} %tok.1, bf16[32,4096]{1,0:T(8,128)(2,1)} %upg.1, bf16[4096,896]{1,0:T(8,128)(2,1)} %wg_h.1, bf16[4096,896]{1,0:T(8,128)(2,1)} %wu_h.1, bf16[896,4096]{1,0:T(8,128)(2,1)} %wd_h.1), custom_call_target="tpu_custom_call" | custom-call | flops 5637144576 | bytes 22020096 | tf_op jit(solution)/shard_map/pallas_call | solution.py:403
  48.0 2.4 %shard_map.69 = (bf16[32,4096]{1,0:T(8,128)(2,1)}, f32[896,512]{1,0:T(8,128)}) custom-call(bf16[32,4096]{1,0:T(8,128)(2,1)} %get-tuple-element.4.tokens_in, f32[896,512]{1,0:T(8,128)} %get-tuple-element.5.down_in), custom_call_target="tpu_custom_call" | custom-call | tf_op jit(solution)/shard_map/pallas_call | solution.py:420

commit v4 on v3

--- a/solution.py
+++ b/solution.py
@@ -92,11 +92,12 @@
     def x_from(o):
         return lax.rem(x + n_x - o, n_x) * 2 + c
 
+    def z_from(o):
+        partner = (z + 1 - 2 * lax.rem(z, 2), lax.rem(z + 2, 4), 3 - z)[o - 1]
+        return partner * 2 + y
+
     def z_to(o):
-        return (lax.rem(z + o, n_z) * 2 + y, t)
-
-    def z_from(o):
-        return lax.rem(z + n_z - o, n_z) * 2 + y
+        return (z_from(o), t)
 
     def dp_to(o):
         return lax.rem(d + o, n_dp)
@@ -257,7 +258,8 @@
             if k > 0:
                 p = gh[fs, :] + p
             gh[fs, :] = p
-        pass_hidden(0, k)
+        if k >= 2:
+            pass_hidden(0, k - 2)
     for o in xs:
         up_x[o].start()
     for f, n in pieces:
@@ -297,12 +299,13 @@
         if q > 0:
             add_cores(q - 1)
         if q == 2:
-            pass_hidden(1, 0)
+            pass_hidden(0, 2)
     add_cores(PARTS - 1)
-    pass_hidden(1, 1)
+    pass_hidden(0, 3)
     for o in xs:
         up_x[o].wait_recv()
         up_f[o].start()
+    pass_hidden(1, 0)
     for q in range(PARTS):
         qs = slice(q * step, (q + 1) * step)
         total = part[of_tensor(t), qs] + pc_in[x, :, qs].astype(F32)
@@ -317,14 +320,12 @@
     for o in xs:
         up_f[o].wait_recv()
     factor = float(n_dp * replica) ** (-0.5)
-    pending = [(s, j) for s in range(n_x) for j in range(len(pieces))]
-    pending = [p for p in pending if p not in ((0, 0), (0, 1), (0, 2), (0, 3), (1, 0), (1, 1))]
-    for p in pending[:1]:
-        pass_hidden(*p)
+    pass_hidden(1, 1)
     for j, (f, n) in enumerate(pieces):
+        if j == 0:
+            pass_hidden(1, 2)
         if j == 1:
-            for p in pending[1:]:
-                pass_hidden(*p)
+            pass_hidden(1, 3)
         for s in range(n_x):
             hid_y[s, j].wait_recv()
             for o in zs:
@@ -373,7 +374,7 @@
     units = w_gate.shape[1]
     mine = width // n_dp
     n_x, n_z = n_tensor // 2, n_dp // 2
-    if rows % 16 or n_tensor % 2 or n_dp % 2 or n_x != 2 or n_z < 2 or len(range(0, units, UNITS)) != PARTS:
+    if rows % 16 or n_tensor % 2 or n_dp % 2 or n_x != 2 or n_z != 4 or len(range(0, units, UNITS)) != PARTS:
         return plain_body(tokens, upstream_grad, w_gate, w_up, w_down)
     replica = rows * n_tensor
     n_pieces = -(-units // UNITS)

time: 51.1 us -> 52.1 us (1.020); the launches traced: 50.4 us -> 52 us
  Pallas kernels: 49.8 us -> 51.3 us
    pallas_call x1, Pallas kernels: 47.4 us -> 48.9 us  [body(): pl.pallas_call(functools.partial(kernel, n_dp, n_tensor), out_shape=(jax....]
where the time goes in v4:
time: 52.1 us; the launch traced here: 52 us
  Pallas kernels  51.3 us (98%)
  between operations  0.64 us (1%)
    pallas_call x1, Pallas kernels, body(): pl.pallas_call(functools.partial(kernel, n_dp, n_tensor), out_shape=(jax....  48.9 us
    pallas_call x1, Pallas kernels, body(): pl.pallas_call(place, out_shape=tuple((jax.ShapeDtypeStruct(g.shape, g.dt...  2.41 us

profile of v4, /device:TPU:0, one launch (start us, length us, event | category | flops | bytes accessed | tf_op | source)
XLA Modules:
  0.0 52.0 jit_solution(3893677511890462688)
XLA Ops:
  0.6 48.9 %shard_map.68 = (bf16[32,4096]{1,0:T(8,128)(2,1)}, f32[896,512]{1,0:T(8,128)}) custom-call(bf16[32,4096]{1,0:T(8,128)(2,1)} %tok.1, bf16[32,4096]{1,0:T(8,128)(2,1)} %upg.1, bf16[4096,896]{1,0:T(8,128)(2,1)} %wg_h.1, bf16[4096,896]{1,0:T(8,128)(2,1)} %wu_h.1, bf16[896,4096]{1,0:T(8,128)(2,1)} %wd_h.1), custom_call_target="tpu_custom_call" | custom-call | flops 5637144576 | bytes 22020096 | tf_op jit(solution)/shard_map/pallas_call | solution.py:404
  49.6 2.4 %shard_map.69 = (bf16[32,4096]{1,0:T(8,128)(2,1)}, f32[896,512]{1,0:T(8,128)}) custom-call(bf16[32,4096]{1,0:T(8,128)(2,1)} %get-tuple-element.4.tokens_in, f32[896,512]{1,0:T(8,128)} %get-tuple-element.5.down_in), custom_call_target="tpu_custom_call" | custom-call | tf_op jit(solution)/shard_map/pallas_call | solution.py:421

commit v5 on v4

--- a/solution.py
+++ b/solution.py
@@ -258,8 +258,7 @@
             if k > 0:
                 p = gh[fs, :] + p
             gh[fs, :] = p
-        if k >= 2:
-            pass_hidden(0, k - 2)
+        pass_hidden(0, k)
     for o in xs:
         up_x[o].start()
     for f, n in pieces:
@@ -299,13 +298,13 @@
         if q > 0:
             add_cores(q - 1)
         if q == 2:
-            pass_hidden(0, 2)
+            pass_hidden(1, 0)
     add_cores(PARTS - 1)
-    pass_hidden(0, 3)
+    pass_hidden(1, 1)
     for o in xs:
         up_x[o].wait_recv()
         up_f[o].start()
-    pass_hidden(1, 0)
+    pass_hidden(1, 2)
     for q in range(PARTS):
         qs = slice(q * step, (q + 1) * step)
         total = part[of_tensor(t), qs] + pc_in[x, :, qs].astype(F32)
@@ -320,12 +319,8 @@
     for o in xs:
         up_f[o].wait_recv()
     factor = float(n_dp * replica) ** (-0.5)
-    pass_hidden(1, 1)
+    pass_hidden(1, 3)
     for j, (f, n) in enumerate(pieces):
-        if j == 0:
-            pass_hidden(1, 2)
-        if j == 1:
-            pass_hidden(1, 3)
         for s in range(n_x):
             hid_y[s, j].wait_recv()
             for o in zs:

time: 52.1 us -> 48.5 us (0.931)
  Pallas kernels: 51.3 us -> 47.7 us
    pallas_call x1, Pallas kernels: 48.9 us -> 45.3 us  [body(): pl.pallas_call(functools.partial(kernel, n_dp, n_tensor), out_shape=(jax....]
where the time goes in v5:
time: 48.5 us; the launch traced here: 48.3 us
  Pallas kernels  47.7 us (98%)
  between operations  0.64 us (1%)
    pallas_call x1, Pallas kernels, body(): pl.pallas_call(functools.partial(kernel, n_dp, n_tensor), out_shape=(jax....  45.3 us
    pallas_call x1, Pallas kernels, body(): pl.pallas_call(place, out_shape=tuple((jax.ShapeDtypeStruct(g.shape, g.dt...  2.41 us

profile of v5, /device:TPU:0, one launch (start us, length us, event | category | flops | bytes accessed | tf_op | source)
XLA Modules:
  0.0 48.3 jit_solution(22833591486253603)
XLA Ops:
  0.6 45.3 %shard_map.68 = (bf16[32,4096]{1,0:T(8,128)(2,1)}, f32[896,512]{1,0:T(8,128)}) custom-call(bf16[32,4096]{1,0:T(8,128)(2,1)} %tok.1, bf16[32,4096]{1,0:T(8,128)(2,1)} %upg.1, bf16[4096,896]{1,0:T(8,128)(2,1)} %wg_h.1, bf16[4096,896]{1,0:T(8,128)(2,1)} %wu_h.1, bf16[896,4096]{1,0:T(8,128)(2,1)} %wd_h.1), custom_call_target="tpu_custom_call" | custom-call | flops 5637144576 | bytes 22020096 | tf_op jit(solution)/shard_map/pallas_call | solution.py:399
  45.9 2.4 %shard_map.69 = (bf16[32,4096]{1,0:T(8,128)(2,1)}, f32[896,512]{1,0:T(8,128)}) custom-call(bf16[32,4096]{1,0:T(8,128)(2,1)} %get-tuple-element.4.tokens_in, f32[896,512]{1,0:T(8,128)} %get-tuple-element.5.down_in), custom_call_target="tpu_custom_call" | custom-call | tf_op jit(solution)/shard_map/pallas_call | solution.py:416

commit v6 on v5

--- a/solution.py
+++ b/solution.py
@@ -96,6 +96,9 @@
         partner = (z + 1 - 2 * lax.rem(z, 2), lax.rem(z + 2, 4), 3 - z)[o - 1]
         return partner * 2 + y
 
+    def z_mirror(o):
+        return z_from(o) + 1 - 2 * y
+
     def z_to(o):
         return (z_from(o), t)
 
@@ -185,6 +188,7 @@
             passed[a, k, o].wait_recv()
 
     hid_y, hid_z, hid_f = {}, {}, {}
+    last = (n_x - 1, len(pieces) - 1)
     for s in range(n_x):
         for j in range(len(pieces)):
             here = hid[j].at[d, of_chip(s), :]
@@ -192,9 +196,11 @@
             for o in zs:
                 hid_z[s, j, o] = remote(
                     here, here, hz_s.at[s, j, o - 1], hz_r.at[s, j, o - 1], z_to(o))
-                there = hid[j].at[z_from(o), of_chip(s), :]
+                there, to = hid[j].at[z_from(o), of_chip(s), :], ypeer
+                if (s, j) == last:
+                    there, to = here, (z_mirror(o), t)
                 hid_f[s, j, o] = remote(
-                    there, there, hf_s.at[s, j, o - 1], hf_r.at[s, j, o - 1], ypeer)
+                    there, there, hf_s.at[s, j, o - 1], hf_r.at[s, j, o - 1], to)
 
     def pass_hidden(s, j):
         for o in zs:
@@ -215,6 +221,8 @@
                 hid[j][d, of_chip(s), :] = (g * jax.nn.sigmoid(g) * u).astype(BF16)
                 for o in zs:
                     hid_z[s, j, o].start()
+                    if (s, j) == last:
+                        hid_f[s, j, o].start()
                 hid_y[s, j].start()
 
     for k in range(PARTS):
@@ -233,6 +241,7 @@
         for o in xs:
             passed[0, k, o].wait_recv()
             forward(o, k)
+    pass_hidden(0, 0)
 
     own[2].wait()
     for copy in exchange:
@@ -258,7 +267,8 @@
             if k > 0:
                 p = gh[fs, :] + p
             gh[fs, :] = p
-        pass_hidden(0, k)
+        if k + 1 < PARTS:
+            pass_hidden(0, k + 1)
     for o in xs:
         up_x[o].start()
     for f, n in pieces:
@@ -319,8 +329,10 @@
     for o in xs:
         up_f[o].wait_recv()
     factor = float(n_dp * replica) ** (-0.5)
-    pass_hidden(1, 3)
     for j, (f, n) in enumerate(pieces):
+        if j == last[1]:
+            for o in zs:
+                hid_z[last[0], j, o].wait_recv()
         for s in range(n_x):
             hid_y[s, j].wait_recv()
             for o in zs:

time: 48.5 us -> 47.8 us (0.986)
  Pallas kernels: 47.7 us -> 47 us
    pallas_call x1, Pallas kernels: 45.3 us -> 44.6 us  [body(): pl.pallas_call(functools.partial(kernel, n_dp, n_tensor), out_shape=(jax....]
where the time goes in v6:
time: 47.8 us; the launch traced here: 47.7 us
  Pallas kernels  47 us (98%)
  between operations  0.64 us (1%)
    pallas_call x1, Pallas kernels, body(): pl.pallas_call(functools.partial(kernel, n_dp, n_tensor), out_shape=(jax....  44.6 us
    pallas_call x1, Pallas kernels, body(): pl.pallas_call(place, out_shape=tuple((jax.ShapeDtypeStruct(g.shape, g.dt...  2.41 us

profile of v6, /device:TPU:0, one launch (start us, length us, event | category | flops | bytes accessed | tf_op | source)
XLA Modules:
  0.0 47.7 jit_solution(2097213752560707676)
XLA Ops:
  0.6 44.6 %shard_map.68 = (bf16[32,4096]{1,0:T(8,128)(2,1)}, f32[896,512]{1,0:T(8,128)}) custom-call(bf16[32,4096]{1,0:T(8,128)(2,1)} %tok.1, bf16[32,4096]{1,0:T(8,128)(2,1)} %upg.1, bf16[4096,896]{1,0:T(8,128)(2,1)} %wg_h.1, bf16[4096,896]{1,0:T(8,128)(2,1)} %wu_h.1, bf16[896,4096]{1,0:T(8,128)(2,1)} %wd_h.1), custom_call_target="tpu_custom_call" | custom-call | flops 5637144576 | bytes 22020096 | tf_op jit(solution)/shard_map/pallas_call | solution.py:411
  45.3 2.4 %shard_map.69 = (bf16[32,4096]{1,0:T(8,128)(2,1)}, f32[896,512]{1,0:T(8,128)}) custom-call(bf16[32,4096]{1,0:T(8,128)(2,1)} %get-tuple-element.4.tokens_in, f32[896,512]{1,0:T(8,128)} %get-tuple-element.5.down_in), custom_call_target="tpu_custom_call" | custom-call | tf_op jit(solution)/shard_map/pallas_call | solution.py:428
